TPU v7x, 1024 devices: a whole 4x8x16 slice. The times are simulated.
1024 devices in a mesh: exp: 16 (over x, z_hi), dp: 64 (over y, z_lo, core).
Axes of the slice: x: 4, y: 8, z: 16 (z_hi: 4, z_lo: 4; z = z_hi * 4 + z_lo), core: 2. Of those that a mesh axis runs over, the one named last changes fastest.
Arguments:
- tokens: bfloat16 [8192, 3584], P('dp', 'exp'), may hold values from -6 to 6
- cotangent: bfloat16 [8192, 3584], P('dp', 'exp'), may hold values from -6 to 6
- expert_ids: int32 [8192, 1], P('dp'), may hold values from 0 to 63; in each aligned block of 128 rows (0 to 127, 128 to 255, ...) at most 4 rows name the same one
- gate_prob: bfloat16 [8192], P('dp'), may hold values from 0.099609375 to 1
- w_gate: bfloat16 [64, 1024, 3584], P('dp', 'exp'), may hold values from -0.09375 to 0.09375
- w_up: bfloat16 [64, 1024, 3584], P('dp', 'exp'), may hold values from -0.09375 to 0.09375
- w_down: bfloat16 [64, 1024, 3584], P('dp', 'exp'), may hold values from -0.1875 to 0.1875
Outputs:
- token_grad: bfloat16 [8192, 3584], P('dp', 'exp')
- prob_grad: float32 [8192], P('dp')
- gate_grad: bfloat16 [64, 1024, 3584], P('dp', 'exp')
- up_grad: bfloat16 [64, 1024, 3584], P('dp', 'exp')
- down_grad: bfloat16 [64, 1024, 3584], P('dp', 'exp')
Inputs may be any that keep to these rules, and one draw needn't show every extreme that they name: `expert_ids`: among the 128 rows of one data shard no expert is named more than 4 times, a bound that some block reaches.
All inputs are finite; a program needn't handle non-finite values.
Results may differ from a plain program's by a relative error of at most 0.005.
Values may be sent and summed in bfloat16 or wider, within the bound.
A program may use at most 32 MiB of HBM per device.

v0:
```python
import jax
import jax.numpy as jnp
from jax import lax
from jax.sharding import PartitionSpec as P


def shards(tokens, cotangent, expert_ids, gate_prob, w_gate, w_up, w_down):
    data_count = lax.axis_size("dp")
    home_rows = tokens.shape[0]
    columns = tokens.shape[1]
    capacity = max(2, 2 * home_rows // data_count)
    slot_count = data_count * capacity
    chosen = expert_ids[:, 0]
    onehot = (chosen[:, None] == jnp.arange(data_count, dtype=jnp.int32)[None, :]).astype(jnp.int32)
    earlier = jnp.cumsum(onehot, axis=0) - onehot
    slot_index = jnp.sum(earlier * onehot, axis=1)
    position = chosen * capacity + slot_index
    placing = (position[None, :] == jnp.arange(slot_count, dtype=jnp.int32)[:, None]).astype(
        jnp.bfloat16
    )
    send_in = jnp.dot(placing, tokens, preferred_element_type=jnp.float32).astype(jnp.bfloat16)
    send_back = jnp.dot(placing, cotangent, preferred_element_type=jnp.float32).astype(jnp.bfloat16)
    send_prob = jnp.dot(placing, gate_prob, preferred_element_type=jnp.float32).astype(jnp.bfloat16)
    recv_in, recv_back, recv_prob = (
        lax.all_to_all(
            send_in.reshape(data_count, capacity, columns),
            "dp",
            split_axis=0,
            concat_axis=0,
            tiled=True,
        ),
        lax.all_to_all(
            send_back.reshape(data_count, capacity, columns),
            "dp",
            split_axis=0,
            concat_axis=0,
            tiled=True,
        ),
        lax.all_to_all(
            send_prob.reshape(data_count, capacity), "dp", split_axis=0, concat_axis=0, tiled=True
        ),
    )
    rows_in = recv_in.reshape(slot_count, columns)
    rows_back = recv_back.reshape(slot_count, columns)
    weight_rows = recv_prob.reshape(slot_count).astype(jnp.float32)[:, None]
    full_in, full_back = (
        lax.all_gather(rows_in, "exp", axis=1, tiled=True),
        lax.all_gather(rows_back, "exp", axis=1, tiled=True),
    )
    gate_panel = w_gate[0]
    up_panel = w_up[0]
    down_panel = w_down[0]
    contract_last = (((1,), (1,)), ((), ()))
    contract_first = (((0,), (0,)), ((), ()))
    gate = lax.dot_general(full_in, gate_panel, contract_last, preferred_element_type=jnp.float32)
    upper = lax.dot_general(full_in, up_panel, contract_last, preferred_element_type=jnp.float32)
    sigmoid_gate = jax.nn.sigmoid(gate)
    hidden = gate * sigmoid_gate * upper
    back_hidden = lax.dot_general(
        full_back, down_panel, contract_last, preferred_element_type=jnp.float32
    )
    prob_grad = lax.psum(jnp.sum(hidden * back_hidden, axis=1), "exp")
    hidden_grad = weight_rows * back_hidden
    up_delta = (hidden_grad * gate * sigmoid_gate).astype(jnp.bfloat16)
    gate_delta = (hidden_grad * upper * sigmoid_gate * (1.0 + gate * (1.0 - sigmoid_gate))).astype(
        jnp.bfloat16
    )
    scaled = (weight_rows * hidden).astype(jnp.bfloat16)
    down_grad = lax.dot_general(
        scaled, full_back, contract_first, preferred_element_type=jnp.float32
    ).astype(jnp.bfloat16)
    gate_grad = lax.dot_general(
        gate_delta, full_in, contract_first, preferred_element_type=jnp.float32
    ).astype(jnp.bfloat16)
    up_grad = lax.dot_general(
        up_delta, full_in, contract_first, preferred_element_type=jnp.float32
    ).astype(jnp.bfloat16)
    token_full = jnp.dot(gate_delta, gate_panel, preferred_element_type=jnp.float32) + jnp.dot(
        up_delta, up_panel, preferred_element_type=jnp.float32
    )
    token_rows = lax.psum_scatter(token_full, "exp", scatter_dimension=1, tiled=True)
    back_rows, back_prob = (
        lax.all_to_all(
            token_rows.reshape(data_count, capacity, columns),
            "dp",
            split_axis=0,
            concat_axis=0,
            tiled=True,
        ),
        lax.all_to_all(
            prob_grad.reshape(data_count, capacity), "dp", split_axis=0, concat_axis=0, tiled=True
        ),
    )
    placing_wide = placing.astype(jnp.float32)
    token_grad = lax.dot_general(
        placing_wide,
        back_rows.reshape(slot_count, columns),
        contract_first,
        precision=lax.Precision.HIGHEST,
        preferred_element_type=jnp.float32,
    ).astype(jnp.bfloat16)
    prob_home = jnp.dot(
        back_prob.reshape(slot_count), placing_wide, precision=lax.Precision.HIGHEST
    )
    return (token_grad, prob_home, gate_grad[None], up_grad[None], down_grad[None])


def solution(mesh):
    in_specs = (
        P("dp", "exp"),
        P("dp", "exp"),
        P("dp", None),
        P("dp"),
        P("dp", "exp", None),
        P("dp", "exp", None),
        P("dp", "exp", None),
    )
    out_specs = (
        P("dp", "exp"),
        P("dp"),
        P("dp", "exp", None),
        P("dp", "exp", None),
        P("dp", "exp", None),
    )
    return jax.shard_map(shards, mesh=mesh, in_specs=in_specs, out_specs=out_specs, check_vma=False)
```

profile of v0, /device:TPU:1, one launch (start us, length us, event | category | flops | bytes accessed | tf_op | source)
XLA Modules:
  0.0 422.3 jit_solution(5508900763121705877)
XLA Ops:
  7.2 0.0 copy-start
  7.2 0.0 copy-start.5
  7.2 0.0 copy-start.6
  7.2 0.0 copy-start.3
  7.2 0.0 all-gather.5.cloned.1.call-start
  7.3 0.8 fusion.18
  8.1 0.2 reduce_window_sum.11
  8.2 0.8 select_reduce_fusion
  9.1 0.7 multiply_add_fusion
  9.7 1.0 convolution_convert_fusion.3
  10.8 0.1 copy.18
  10.9 28.3 %all_to_all.34 = bf16[64,4,224]{2,1,0:T(4,128)(2,1)S(1)} all-to-all(bf16[64,4,224]{2,1,0:T(4,128)(2,1)S(1)} %reshape.59), channel_id=1, replica_groups=mesh['exp'=16,'dp'=64] {'dp'}, dimensions={0} | all-to-all | bytes 229376 | tf_op jit(solution)/shard_map/all_to_all | solution.py:25
  39.2 0.1 reshape.60
  39.3 0.8 copy.19
  40.1 0.0 all-gather.5.cloned.1.call-update
  40.1 0.0 all-gather.3.cloned.1.call-start
  40.2 0.0 copy-done.5
  40.2 0.2 convolution_convert_fusion.4
  40.4 0.1 copy.16
  40.5 14.7 %all_to_all.35 = bf16[64,4,224]{2,1,0:T(4,128)(2,1)S(1)} all-to-all(bf16[64,4,224]{2,1,0:T(4,128)(2,1)S(1)} %reshape.57), channel_id=1, replica_groups=mesh['exp'=16,'dp'=64] {'dp'}, dimensions={0} | all-to-all | bytes 229376 | tf_op jit(solution)/shard_map/all_to_all | solution.py:32
  55.2 0.1 reshape.58
  55.3 0.8 copy.17
  56.1 0.0 all-gather.3.cloned.1.call-update
  56.1 0.0 reduce-scatter.2.cloned.1.call-start
  56.1 0.0 copy-done.6
  56.2 0.1 fusion.12
  56.3 0.1 all_to_all.28
  56.4 13.5 %all_to_all.36 = bf16[64,1,4]{2,1,0:T(2,128)(2,1)S(1)} all-to-all(bf16[64,1,4]{2,1,0:T(2,128)(2,1)S(1)} %all_to_all.28), channel_id=1, replica_groups=mesh['exp'=16,'dp'=64] {'dp'}, dimensions={0} | all-to-all | bytes 1024 | tf_op jit(solution)/shard_map/all_to_all | solution.py:39
  69.9 0.1 convert_reduce_fusion
  70.0 0.1 reshape.64
  70.1 0.0 copy-start.4
  70.2 63.7 %all-gather.5.cloned.1.call-done = bf16[256,3584]{0,1:T(8,128)(2,1)} async-done(((bf16[256,224]{0,1:T(8,128)(2,1)}), bf16[256,3584]{0,1:T(8,128)(2,1)}) %all-gather.5.cloned.1.call-update) | async-done | bytes 1835024 | tf_op jit(solution)/shard_map/all_gather | solution.py:47
  133.8 0.0 copy-done.3
  133.8 0.0 copy-start.1
  133.8 2.1 fusion.8
  135.9 0.0 copy-done
  135.9 0.0 copy-done.1
  135.9 0.4 fusion.5
  136.4 93.4 %all-gather.3.cloned.1.call-done = bf16[256,3584]{0,1:T(8,128)(2,1)} async-done(((bf16[256,224]{0,1:T(8,128)(2,1)}), bf16[256,3584]{0,1:T(8,128)(2,1)}) %all-gather.3.cloned.1.call-update) | async-done | bytes 1835024 | tf_op jit(solution)/shard_map/all_gather | solution.py:48
  229.7 0.0 copy-done.4
  229.7 2.0 multiply_reduce_fusion
  231.7 0.7 fusion.3
  232.4 2.5 convolution_add_fusion
  234.9 0.0 reduce-scatter.2.cloned.1.call-update
  234.9 0.1 all_to_all.26
  235.0 88.0 %psum.7 = f32[64,1,4]{2,0,1:T(8,128)} all-reduce(f32[64,1,4]{2,0,1:T(8,128)S(1)} %all_to_all.26), channel_id=1, replica_groups=mesh['exp'=16,'dp'=64] {'exp'}, use_global_device_ids=true, to_apply=%region_4.5 | all-reduce | flops 256 | bytes 2048 | tf_op jit(solution)/shard_map/psum | solution.py:62
  323.1 29.5 %all-to-all-start.4 = ((f32[64,1,4]{2,1,0:T(1,128)}), f32[64,1,4]{2,1,0:T(1,128)S(1)}, u32[]{:S(2)}, u32[]{:S(2)}) async-start(f32[64,1,4]{2,1,0:T(1,128)} %bitcast.6), calls=%async_computation.5 | async-start | bytes 65536 | tf_op jit(solution)/shard_map/all_to_all | solution.py:90
  352.5 35.9 %reduce-scatter.2.cloned.1.call-done = f32[256,224]{0,1:T(8,128)} async-done(((f32[256,3584]{0,1:T(8,128)}), f32[256,224]{0,1:T(8,128)}) %reduce-scatter.2.cloned.1.call-update) | async-done | bytes 229392 | tf_op jit(solution)/shard_map/reduce_scatter | solution.py:81
  388.4 1.1 copy.20
  389.5 0.8 reshape.61
  390.3 0.0 all-to-all-done.4
  390.3 10.9 %all-to-all-start.3 = ((f32[64,4,224]{2,1,0:T(4,128)}), f32[64,4,224]{2,1,0:T(4,128)S(1)}, u32[]{:S(2)}, u32[]{:S(2)}) async-start(f32[64,4,224]{2,1,0:T(4,128)} %reshape.61), calls=%async_computation.4 | async-start | bytes 524288 | tf_op jit(solution)/shard_map/all_to_all | solution.py:83
  401.1 0.0 copy-start.2
  401.1 1.4 fusion
  402.6 1.4 fusion.1
  404.0 0.0 copy-done.2
  404.0 1.4 fusion.2
  405.5 0.5 broadcast.27
  406.0 0.7 reduce.7
  406.7 0.1 reshape.67
  406.8 0.7 convolution_bitcast_fusion
  407.5 7.1 %all-to-all-done.3 = f32[64,4,224]{2,1,0:T(4,128)S(1)} async-done(((f32[64,4,224]{2,1,0:T(4,128)}), f32[64,4,224]{2,1,0:T(4,128)S(1)}, u32[]{:S(2)}, u32[]{:S(2)}) %all-to-all-start.3) | async-done | bytes 229408 | tf_op jit(solution)/shard_map/all_to_all | solution.py:83
  414.7 0.1 reshape.62
  414.8 1.0 convolution_convert_fusion.5
  (3 shorter events, 0.1 us)
Async XLA Ops:
  7.2 128.7 %copy-start = (bf16[1,64,3584]{2,1,0:T(8,128)(2,1)S(1)}, bf16[1,64,3584]{2,1,0:T(8,128)(2,1)}, u32[]{:S(2)}) copy-start(bf16[1,64,3584]{2,1,0:T(8,128)(2,1)} %param.11) | copy-start | bytes 1376260
  7.2 33.0 %copy-start.5 = (bf16[128,224]{0,1:T(8,128)(2,1)S(1)}, bf16[128,224]{0,1:T(8,128)(2,1)}, u32[]{:S(2)}) copy-start(bf16[128,224]{0,1:T(8,128)(2,1)} %param.8) | copy-start | bytes 172036
  7.2 49.0 %copy-start.6 = (bf16[128]{0:T(256)(128)(2,1)S(1)}, bf16[128]{0:T(256)(128)(2,1)}, u32[]{:S(2)}) copy-start(bf16[128]{0:T(256)(128)(2,1)} %param.10) | copy-start | bytes 772
  7.2 126.6 %copy-start.3 = (bf16[1,64,3584]{2,1,0:T(8,128)(2,1)S(1)}, bf16[1,64,3584]{2,1,0:T(8,128)(2,1)}, u32[]{:S(2)}) copy-start(bf16[1,64,3584]{2,1,0:T(8,128)(2,1)} %param.12) | copy-start | bytes 1376260
  7.2 126.6 %all-gather.5.cloned.1.call-start = ((), (), s32[]{:S(2)}) async-start(), calls=%async_computation.7 | async-start | bytes 1949696 | tf_op jit(solution)/shard_map/all_gather | solution.py:47
  40.1 189.6 %all-gather.3.cloned.1.call-start = ((), (), s32[]{:S(2)}) async-start(), calls=%async_computation.6 | async-start | bytes 1949696 | tf_op jit(solution)/shard_map/all_gather | solution.py:48
  56.1 332.3 %reduce-scatter.2.cloned.1.call-start = ((), (), s32[]{:S(2)}) async-start(), calls=%async_computation.8 | async-start | bytes 3899392 | tf_op jit(solution)/shard_map/reduce_scatter | solution.py:81
  70.1 159.6 %copy-start.4 = (bf16[1,64,3584]{2,1,0:T(8,128)(2,1)S(1)}, bf16[1,64,3584]{2,1,0:T(8,128)(2,1)}, u32[]{:S(2)}) copy-start(bf16[1,64,3584]{2,1,0:T(8,128)(2,1)} %param.13) | copy-start | bytes 1376260
  133.8 2.1 copy-start.1
  323.1 67.2 %all-to-all-start.4 = ((f32[64,1,4]{2,1,0:T(1,128)}), f32[64,1,4]{2,1,0:T(1,128)S(1)}, u32[]{:S(2)}, u32[]{:S(2)}) async-start(f32[64,1,4]{2,1,0:T(1,128)} %bitcast.6), calls=%async_computation.5 | async-start | bytes 65536 | tf_op jit(solution)/shard_map/all_to_all | solution.py:90
  390.3 24.4 %all-to-all-start.3 = ((f32[64,4,224]{2,1,0:T(4,128)}), f32[64,4,224]{2,1,0:T(4,128)S(1)}, u32[]{:S(2)}, u32[]{:S(2)}) async-start(f32[64,4,224]{2,1,0:T(4,128)} %reshape.61), calls=%async_computation.4 | async-start | bytes 524288 | tf_op jit(solution)/shard_map/all_to_all | solution.py:83
  401.1 2.9 copy-start.2
Sparse Core Ops, SparseCore 0:
  40.2 93.5 all-gather.4
  138.6 91.0 all-gather.2
  235.2 153.2 reduce-scatter.1
where the time goes:
time: 423 us; the launch traced here: 422 us
  waiting for transfers between devices  200 us (47%)
  blocking collectives  145 us (34%)
  starting transfers between devices  40.4 us (10%)
  matrix products  15 us (4%)
  between operations  14 us (3%)
  local copies, waits for them, and re-layouts  4.86 us (1%)
    all_gather x1, waiting for transfers between devices, shards(): lax.all_gather(rows_back, 'exp', axis=1, tiled=True)  93.4 us
    psum x1, blocking collectives, shards(): prob_grad = lax.psum(jnp.sum(hidden * back_hidden, axis=1), 'exp')  88 us
    all_gather x1, waiting for transfers between devices, shards(): lax.all_gather(rows_in, 'exp', axis=1, tiled=True)  63.7 us
    reduce_scatter x1, waiting for transfers between devices, shards(): lax.psum_scatter(token_full, 'exp', scatter_dimension=1, tiled=True)  35.9 us
    all_to_all x1, starting transfers between devices, shards(): lax.all_to_all(prob_grad.reshape(data_count, capacity), 'dp', split_axis=...  29.5 us
    all_to_all x1, blocking collectives, shards(): lax.all_to_all(send_in.reshape(data_count, capacity, columns), 'dp', spli...  28.3 us
    all_to_all x1, blocking collectives, shards(): lax.all_to_all(send_back.reshape(data_count, capacity, columns), 'dp', sp...  14.7 us
    all_to_all x1, blocking collectives, shards(): lax.all_to_all(send_prob.reshape(data_count, capacity), 'dp', split_axis=...  13.5 us
  transfers between devices with their start and end apart: 5, of which 4 were waited for; matrix products, arithmetic and copies ran while one was open for 3% of the time, Pallas kernels for 0%

commit v1 on v0

v1 whole, which is shorter than its diff:
```python
import functools

import jax
import jax.numpy as jnp
from jax import lax
from jax.experimental import pallas as pl
from jax.experimental.pallas import tpu as pltpu
from jax.sharding import PartitionSpec as P

MESH = pl.DeviceIdType.MESH
BF = jnp.bfloat16
F32 = jnp.float32
NT = (((1,), (1,)), ((), ()))
NN = (((1,), (0,)), ((), ()))
TN = (((0,), (0,)), ((), ()))


def iota(shape, dim):
    return lax.broadcasted_iota(jnp.int32, shape, dim)


def dot(a, b, dims):
    return lax.dot_general(a, b, dims, preferred_element_type=F32)


def pack(left, right):
    lane = iota((192, 128), 1)
    tail = right[192:256]
    moved = jnp.concatenate([pltpu.roll(tail, 96, 1), pltpu.roll(tail, 64, 1), pltpu.roll(tail, 32, 1)], axis=0)
    return jnp.concatenate([left, jnp.where(lane < 96, right[0:192], moved)], axis=0)


def unpack(packed):
    lane = iota((192, 128), 1)
    low = iota((64, 128), 1)
    rest = packed[256:448]
    top = jnp.where(lane < 96, rest, 0.0)
    tail = jnp.where(
        low < 32,
        pltpu.roll(rest[0:64], 32, 1),
        jnp.where(
            low < 64,
            pltpu.roll(rest[64:128], 64, 1),
            jnp.where(low < 96, pltpu.roll(rest[128:192], 96, 1), 0.0),
        ),
    )
    return packed[0:256], jnp.concatenate([top, tail], axis=0)


def shift_left(a, b, count):
    lane = iota(a.shape, 1)
    return jnp.where(lane < 128 - count, pltpu.roll(a, 128 - count, 1), pltpu.roll(b, 128 - count, 1))


def kernel(
    n_dp,
    ids_ref, prob_ref, tok_ref, cot_ref, wg_ref, wu_ref, wd_ref,
    tg_ref, pg_ref, gg_ref, ug_ref, dg_ref,
    sbuf, rbuf, zbuf, wbuf, wpad, tpad, full, gusend, gurecv, bsend, brecv, scal, delt,
    pbx, pbz, pxr, pzr, rs1s, rs1r, rs2s, rs2r, rets, retr, gradb, ssem, rsem, lsem,
):
    exp = lax.axis_index("exp")
    me = lax.axis_index("dp")
    x, z = exp // 4, exp % 4
    xs = [(x + k) % 4 for k in range(4)]
    zs = [(z + k) % 4 for k in range(4)]

    def x_dev(k):
        return {"exp": xs[k] * 4 + z, "dp": me}

    def z_dev(k):
        return {"exp": x * 4 + zs[k], "dp": me}

    counter = [0]

    def remote(src, dst, dev):
        i = counter[0]
        counter[0] += 1
        return pltpu.make_async_remote_copy(
            src_ref=src, dst_ref=dst, send_sem=ssem.at[i], recv_sem=rsem.at[i],
            device_id=dev, device_id_type=MESH,
        )

    pending = []

    def start(copy):
        copy.start()
        pending.append(copy)
        return copy

    barrier = pltpu.get_barrier_semaphore()

    def greet(k, carry):
        pl.semaphore_signal(barrier, inc=1, device_id={"exp": exp, "dp": (me + k) % n_dp}, device_id_type=MESH)
        return carry

    lax.fori_loop(1, n_dp, greet, 0)
    for k in range(1, 4):
        pl.semaphore_signal(barrier, inc=1, device_id=x_dev(k), device_id_type=MESH)
        pl.semaphore_signal(barrier, inc=1, device_id=z_dev(k), device_id_type=MESH)

    own_w = []
    for a, ref in enumerate((wg_ref, wu_ref, wd_ref)):
        copy = pltpu.make_async_copy(
            ref.at[:, pl.ds(pl.multiple_of(x * 896, 128), 896)], wbuf.at[a, x], lsem.at[a]
        )
        copy.start()
        own_w.append(copy)

    ids = ids_ref[...]
    hot = (iota((n_dp, 128), 0) == ids).astype(F32)
    before = (iota((128, 128), 0) < iota((128, 128), 1)).astype(BF)
    earlier = dot(hot.astype(BF), before, NN)
    slot = jnp.sum(hot * earlier, axis=0, keepdims=True)
    position = ids.astype(F32) * 4.0 + slot

    rows = iota((16 * n_dp, 128), 0)
    row_slot = ((rows >> 4) * 4 + (rows & 3)).astype(F32)
    row_part = (rows >> 2) & 3
    placing = jnp.where(row_slot == position, 1.0, 0.0).astype(BF)
    prob_block = jnp.where(iota((32, 128), 0) == 0, prob_ref[...].astype(F32), 0.0).astype(BF)
    out = dot(placing, tok_ref[0:128], NT)
    out = jnp.where(row_part == 1, dot(placing, jnp.concatenate([tok_ref[128:224], prob_block], axis=0), NT), out)
    out = jnp.where(row_part == 2, dot(placing, cot_ref[0:128], NT), out)
    zero_block = jnp.zeros((32, 128), BF)
    out = jnp.where(row_part == 3, dot(placing, jnp.concatenate([cot_ref[128:224], zero_block], axis=0), NT), out)
    sbuf[...] = out.astype(BF).reshape(n_dp, 16, 128)

    pl.semaphore_wait(barrier, n_dp - 1 + 6)

    i_disp = counter[0]
    counter[0] += 1

    def send(k, carry):
        to = (me + k) % n_dp
        pltpu.make_async_remote_copy(
            src_ref=sbuf.at[to], dst_ref=rbuf.at[me], send_sem=ssem.at[i_disp], recv_sem=rsem.at[i_disp],
            device_id={"exp": exp, "dp": to}, device_id_type=MESH,
        ).start()
        return carry

    lax.fori_loop(1, n_dp, send, 0)
    rbuf[me] = sbuf[me]

    w_copies = [
        [
            start(remote(
                ref.at[:, pl.ds(pl.multiple_of(xs[k] * 896, 128), 896)], wbuf.at[a, x], x_dev(k)
            ))
            for k in range(1, 4)
        ]
        for a, ref in enumerate((wg_ref, wu_ref, wd_ref))
    ]

    dispatched = pltpu.make_async_remote_copy(
        src_ref=sbuf.at[pl.ds(0, n_dp - 1)], dst_ref=rbuf.at[pl.ds(0, n_dp - 1)],
        send_sem=ssem.at[i_disp], recv_sem=rsem.at[i_disp], device_id={"exp": exp, "dp": me}, device_id_type=MESH,
    )
    dispatched.wait_recv()

    o, i = iota((256, 256), 0), iota((256, 256), 1)
    order = jnp.where(i == ((o >> 2) & 15) * 16 + (o >> 6) * 4 + (o & 3), 1.0, 0.0).astype(BF)
    groups = []
    for g in range(n_dp // 16):
        groups.append(dot(order, rbuf[16 * g:16 * g + 16].reshape(256, 128), NN))
    parts = [jnp.concatenate([group[64 * j:64 * j + 64] for group in groups], axis=0) for j in range(4)]
    pick = jnp.where((iota((8, 128), 0) == 0) & (iota((8, 128), 1) == 96), 1.0, 0.0).astype(BF)
    weight = dot(pick, parts[1].astype(BF), NT)[0:1]

    def gather_start(a):
        mine = zbuf.at[a, z]
        halves = [mine.at[pl.ds(0, 224)], mine.at[pl.ds(224, 224)]]
        right = [remote(halves[0], halves[0], z_dev(1)), remote(halves[1], halves[1], z_dev(1))]
        left = [remote(halves[1], halves[1], z_dev(3)), remote(halves[0], halves[0], z_dev(3))]
        for n in range(2):
            start(right[n])
            start(left[n])
        return right, left

    def gather_forward(a, right, left):
        from_left = zbuf.at[a, zs[3], pl.ds(0, 224)]
        from_right = zbuf.at[a, zs[1], pl.ds(224, 224)]
        onward_right = remote(from_left, from_left, z_dev(1))
        onward_left = remote(from_right, from_right, z_dev(3))
        right[0].wait_recv()
        start(onward_right)
        left[0].wait_recv()
        start(onward_left)
        return [right[1], left[1], onward_right, onward_left]

    zbuf[0, z] = pack(parts[0], parts[1]).astype(BF)
    t_right, t_left = gather_start(0)
    zbuf[1, z] = pack(parts[2], parts[3]).astype(BF)
    t_rest = gather_forward(0, t_right, t_left)
    for copy in t_right + t_left:
        copy.wait_send()
    pending[:] = [copy for copy in pending if not any(copy is done for done in t_right + t_left)]
    c_right, c_left = gather_start(1)

    def shift_weights(a):
        own_w[a].wait()
        for copy in w_copies[a]:
            copy.wait_recv()
        whole = wbuf[a].reshape(256, 896)
        block = [whole[:, 128 * b:128 * b + 128].astype(F32) for b in range(7)]
        wpad[a, 0] = whole[:, 0:256]
        for n, (first, count) in enumerate(((1, 96), (3, 64), (5, 32))):
            wpad[a, n + 1, :, 0:128] = shift_left(block[first], block[first + 1], count).astype(BF)
            last = block[first + 2] if first + 2 < 7 else block[first + 1]
            wpad[a, n + 1, :, 128:256] = shift_left(block[first + 1], last, count).astype(BF)

    def unpack_all(a):
        for n in range(4):
            left, right = unpack(zbuf[a, n].astype(F32))
            tpad[a, n, :, 0:128] = left.astype(BF)
            tpad[a, n, :, 128:256] = right.astype(BF)

    def join_all(a):
        part = [[tpad[a, n, :, 128 * h:128 * h + 128].astype(F32) for h in range(2)] for n in range(4)]
        nothing = jnp.zeros((256, 128), F32)
        block = [nothing] * 7
        block[0], block[1] = part[0]
        for n, (first, count) in enumerate(((1, 96), (3, 64), (5, 32))):
            lo, hi = part[n + 1]
            block[first] += shift_left(nothing, lo, 128 - count)
            block[first + 1] += shift_left(lo, hi, 128 - count)
            if first + 2 < 7:
                block[first + 2] += shift_left(hi, nothing, 128 - count)
        for b in range(7):
            full[a, :, 128 * b:128 * b + 128] = block[b].astype(BF)

    def project(a, t):
        total = dot(wpad[a, 0], tpad[t, 0], NT)
        for n in range(1, 4):
            total += dot(wpad[a, n], tpad[t, n], NT)
        return total.reshape(4, 64, 256)

    shift_weights(0)
    shift_weights(1)
    for copy in t_rest:
        copy.wait_recv()
    unpack_all(0)
    gusend[:, 0] = project(0, 0)
    gusend[:, 1] = project(1, 0)
    gu_copies = [start(remote(gusend.at[xs[k]], gurecv.at[k - 1], x_dev(k))) for k in range(1, 4)]
    shift_weights(2)
    c_rest = gather_forward(1, c_right, c_left)
    for copy in gu_copies:
        copy.wait_recv()
    gate = gusend[x, 0] + gurecv[0, 0] + gurecv[1, 0] + gurecv[2, 0]
    upper = gusend[x, 1] + gurecv[0, 1] + gurecv[1, 1] + gurecv[2, 1]
    sigmoid = jax.nn.sigmoid(gate)
    hidden = gate * sigmoid * upper
    scal[x] = (weight * hidden).astype(BF)
    s_copies = [start(remote(scal.at[x], scal.at[x], x_dev(k))) for k in range(1, 4)]
    join_all(0)

    for copy in c_rest:
        copy.wait_recv()
    unpack_all(1)
    bsend[...] = project(2, 1)
    b_copies = [start(remote(bsend.at[xs[k]], brecv.at[k - 1], x_dev(k))) for k in range(1, 4)]
    join_all(1)

    def grad_send(a, lhs, t, ref):
        gradb[a] = dot(lhs.reshape(256, 256), full[t], NN).astype(BF).reshape(4, 64, 896)
        return [
            start(remote(gradb.at[a, xs[k]], ref.at[:, pl.ds(pl.multiple_of(x * 896, 128), 896)], x_dev(k)))
            for k in range(1, 4)
        ]

    for copy in b_copies:
        copy.wait_recv()
    back = bsend[x] + brecv[0] + brecv[1] + brecv[2]
    grad = weight * back
    delt[0, x] = (grad * upper * sigmoid * (1.0 + gate * (1.0 - sigmoid))).astype(BF)
    delt[1, x] = (grad * gate * sigmoid).astype(BF)
    d_copies = [start(remote(delt.at[:, x], delt.at[:, x], x_dev(k))) for k in range(1, 4)]
    pbx[...] = jnp.broadcast_to(jnp.sum(hidden * back, axis=0, keepdims=True), (8, 256))
    px_copies = [start(remote(pbx, pxr.at[k - 1], x_dev(k))) for k in range(1, 4)]

    for copy in s_copies:
        copy.wait_recv()
    g_copies = grad_send(2, scal[...], 1, dg_ref)

    for copy in d_copies:
        copy.wait_recv()
    gate_delta = delt[0].reshape(256, 256)
    up_delta = delt[1].reshape(256, 256)

    def token_part(n):
        total = dot(gate_delta, wpad[0, n], TN) + dot(up_delta, wpad[1, n], TN)
        return pack(total[:, 0:128], total[:, 128:256])

    far = token_part(zs[2]).astype(BF)
    rs1s[...] = far.reshape(2, 224, 128)
    r1 = [start(remote(rs1s.at[0], rs1r.at[0], z_dev(1))), start(remote(rs1s.at[1], rs1r.at[1], z_dev(3)))]
    to_right = token_part(zs[1])
    rs2s[0, 1] = to_right[224:448].astype(BF)
    r2 = [start(remote(rs2s.at[0, 1], rs2r.at[0, 1], z_dev(1)))]
    to_left = token_part(zs[3])
    rs2s[1, 0] = to_left[0:224].astype(BF)
    r2.append(start(remote(rs2s.at[1, 0], rs2r.at[1, 0], z_dev(3))))
    for copy in px_copies:
        copy.wait_recv()
    pbz[...] = pbx[...] + pxr[0] + pxr[1] + pxr[2]
    pz_copies = [start(remote(pbz, pzr.at[k - 1], z_dev(k))) for k in range(1, 4)]
    r1[0].wait_recv()
    rs2s[0, 0] = (to_right[0:224] + rs1r[0].astype(F32)).astype(BF)
    r2.append(start(remote(rs2s.at[0, 0], rs2r.at[0, 0], z_dev(1))))
    r1[1].wait_recv()
    rs2s[1, 1] = (to_left[224:448] + rs1r[1].astype(F32)).astype(BF)
    r2.append(start(remote(rs2s.at[1, 1], rs2r.at[1, 1], z_dev(3))))

    g_copies += grad_send(0, delt[0], 0, gg_ref)
    g_copies += grad_send(1, delt[1], 0, ug_ref)
    here = token_part(z)
    for copy in pz_copies:
        copy.wait_recv()
    prob_total = (pbz[...] + pzr[0] + pzr[1] + pzr[2])[0:1]
    first = prob_total.astype(BF).astype(F32)
    second = (prob_total - first).astype(BF).astype(F32)
    third = prob_total - first - second
    eight = iota((8, 256), 0)
    terms = jnp.where(eight == 0, first, jnp.where(eight == 1, second, jnp.where(eight == 2, third, 0.0))).astype(BF)
    into = jnp.where(
        (iota((8, 128), 0) < 3) & (iota((8, 128), 1) == iota((8, 128), 0) + 96), 1.0, 0.0
    ).astype(BF)
    prob_lanes = dot(terms, into, TN)
    o, i = iota((128, 128), 0), iota((128, 128), 1)
    back_order = jnp.where(i == ((o >> 2) & 1) * 64 + (o >> 3) * 4 + (o & 3), 1.0, 0.0).astype(BF)

    for copy in r2:
        copy.wait_recv()
    both = rs2r[0].astype(F32) + rs2r[1].astype(F32)
    left, right = unpack(here + both.reshape(448, 128))
    left = left.astype(BF)
    right = (right + prob_lanes).astype(BF)
    for g in range(n_dp // 16):
        piece = jnp.concatenate([left[64 * g:64 * g + 64], right[64 * g:64 * g + 64]], axis=0)
        rets[16 * g:16 * g + 16] = dot(back_order, piece, NN).reshape(16, 8, 128)

    i_ret = counter[0]
    counter[0] += 1

    def send_back(k, carry):
        to = (me + k) % n_dp
        pltpu.make_async_remote_copy(
            src_ref=rets.at[to], dst_ref=retr.at[me], send_sem=ssem.at[i_ret], recv_sem=rsem.at[i_ret],
            device_id={"exp": exp, "dp": to}, device_id_type=MESH,
        ).start()
        return carry

    lax.fori_loop(1, n_dp, send_back, 0)
    retr[me] = rets[me]
    for a, ref in ((2, dg_ref), (0, gg_ref), (1, ug_ref)):
        ref[:, pl.ds(pl.multiple_of(x * 896, 128), 896)] = gradb[a, x]
    rows = iota((8 * n_dp, 128), 0)
    match = ((rows >> 3) * 4 + (rows & 3)).astype(F32) == position
    part = (rows >> 2) & 1
    returned = pltpu.make_async_remote_copy(
        src_ref=rets.at[pl.ds(0, n_dp - 1)], dst_ref=retr.at[pl.ds(0, n_dp - 1)],
        send_sem=ssem.at[i_ret], recv_sem=rsem.at[i_ret], device_id={"exp": exp, "dp": me}, device_id_type=MESH,
    )
    returned.wait_recv()
    arrived = retr[...].reshape(8 * n_dp, 128)
    small = arrived.astype(BF)
    tg_ref[0:128] = dot(small, jnp.where(match & (part == 0), 1.0, 0.0).astype(BF), TN).astype(BF)
    tg_ref[128:224] = dot(small, jnp.where(match & (part == 1), 1.0, 0.0).astype(BF), TN)[0:96].astype(BF)
    column = arrived[:, 96:97] + arrived[:, 97:98] + arrived[:, 98:99]
    pg_ref[...] = jnp.sum(jnp.where(match & (part == 1), column, 0.0), axis=0, keepdims=True)

    for copy in g_copies:
        copy.wait_recv()
    dispatched.wait_send()
    returned.wait_send()
    for copy in pending:
        copy.wait_send()


def shards(tokens, cotangent, expert_ids, gate_prob, w_gate, w_up, w_down):
    n_dp = lax.axis_size("dp")
    vmem = pl.BlockSpec(memory_space=pltpu.VMEM)
    hbm = pl.BlockSpec(memory_space=pl.ANY)
    grad = jax.ShapeDtypeStruct((64, 3584), BF)
    token_grad, prob_grad, gate_grad, up_grad, down_grad = pl.pallas_call(
        functools.partial(kernel, n_dp),
        out_shape=(
            jax.ShapeDtypeStruct((224, 128), BF),
            jax.ShapeDtypeStruct((1, 128), F32),
            grad, grad, grad,
        ),
        in_specs=[vmem] * 4 + [hbm] * 3,
        out_specs=[vmem] * 5,
        scratch_shapes=[
            pltpu.VMEM((n_dp, 16, 128), BF),
            pltpu.VMEM((n_dp, 16, 128), BF),
            pltpu.VMEM((2, 4, 448, 128), BF),
            pltpu.VMEM((3, 4, 64, 896), BF),
            pltpu.VMEM((3, 4, 256, 256), BF),
            pltpu.VMEM((2, 4, 256, 256), BF),
            pltpu.VMEM((2, 256, 896), BF),
            pltpu.VMEM((4, 2, 64, 256), F32),
            pltpu.VMEM((3, 2, 64, 256), F32),
            pltpu.VMEM((4, 64, 256), F32),
            pltpu.VMEM((3, 64, 256), F32),
            pltpu.VMEM((4, 64, 256), BF),
            pltpu.VMEM((2, 4, 64, 256), BF),
            pltpu.VMEM((8, 256), F32),
            pltpu.VMEM((8, 256), F32),
            pltpu.VMEM((3, 8, 256), F32),
            pltpu.VMEM((3, 8, 256), F32),
            pltpu.VMEM((2, 224, 128), BF),
            pltpu.VMEM((2, 224, 128), BF),
            pltpu.VMEM((2, 2, 224, 128), BF),
            pltpu.VMEM((2, 2, 224, 128), BF),
            pltpu.VMEM((n_dp, 8, 128), F32),
            pltpu.VMEM((n_dp, 8, 128), F32),
            pltpu.VMEM((3, 4, 64, 896), BF),
            pltpu.SemaphoreType.DMA((64,)),
            pltpu.SemaphoreType.DMA((64,)),
            pltpu.SemaphoreType.DMA((3,)),
        ],
        compiler_params=pltpu.CompilerParams(
            collective_id=0, has_side_effects=True, vmem_limit_bytes=48 * 1024 * 1024
        ),
    )(
        expert_ids.reshape(1, -1), gate_prob.reshape(1, -1), tokens.T, cotangent.T, w_gate[0], w_up[0], w_down[0]
    )
    return token_grad.T, prob_grad.reshape(-1), gate_grad[None], up_grad[None], down_grad[None]


def solution(mesh):
    in_specs = (
        P("dp", "exp"),
        P("dp", "exp"),
        P("dp", None),
        P("dp"),
        P("dp", "exp", None),
        P("dp", "exp", None),
        P("dp", "exp", None),
    )
    out_specs = (
        P("dp", "exp"),
        P("dp"),
        P("dp", "exp", None),
        P("dp", "exp", None),
        P("dp", "exp", None),
    )
    return jax.shard_map(shards, mesh=mesh, in_specs=in_specs, out_specs=out_specs, check_vma=False)
```

time: 423 us -> 117 us (0.28)
  waiting for transfers between devices: 200 us -> 0 us
  blocking collectives: 145 us -> 0 us
  Pallas kernels: 0 us -> 107 us
  starting transfers between devices: 40.4 us -> 0 us
  matrix products: 15 us -> 0 us
  between operations: 14 us -> 0.67 us
    all_gather x2 -> x0, waiting for transfers between devices: 157 us -> none  [the longest x1 93.4 us: shards(): lax.all_gather(rows_back, 'exp', axis=1, tiled=True)]
    pallas_call x0 -> x1, Pallas kernels: none -> 107 us  [shards(): pl.pallas_call(functools.partial(kernel, n_dp), out_shape=(jax.ShapeDtype...]
    psum x1 -> x0, blocking collectives: 88 us -> none  [shards(): prob_grad = lax.psum(jnp.sum(hidden * back_hidden, axis=1), 'exp')]
    all_to_all x3 -> x0, blocking collectives: 56.6 us -> none  [the longest x1 28.3 us: shards(): lax.all_to_all(send_in.reshape(data_count, capacity, columns), 'dp', spli...]
    all_to_all x2 -> x0, starting transfers between devices: 40.3 us -> none  [the longest x1 29.5 us: shards(): lax.all_to_all(prob_grad.reshape(data_count, capacity), 'dp', split_axis=...]
    reduce_scatter x1 -> x0, waiting for transfers between devices: 35.9 us -> none  [shards(): lax.psum_scatter(token_full, 'exp', scatter_dimension=1, tiled=True)]
    dot_general x13 -> x0, matrix products: 15 us -> none  [the longest x1 2.49 us: shards(): jnp.dot(up_delta, up_panel, preferred_element_type=jnp.float32)]
    unnamed x14 -> x19, local copies, waits for them, and re-layouts: 0.04 us -> 8.78 us
  transfers between devices with their start and end apart: 5 -> 0, of which waited for: 4 -> 0; matrix products, arithmetic and copies ran while one was open for 3% -> 0% of each run, Pallas kernels for 0% -> 0%
where the time goes in v1:
time: 117 us
  Pallas kernels  107 us (91%)
  local copies, waits for them, and re-layouts  8.78 us (8%)
    pallas_call x1, Pallas kernels, shards(): pl.pallas_call(functools.partial(kernel, n_dp), out_shape=(jax.ShapeDtype...  107 us
    unnamed x19, local copies, waits for them, and re-layouts  8.78 us

profile of v1, /device:TPU:1, one launch (start us, length us, event | category | flops | bytes accessed | tf_op | source)
XLA Modules:
  0.0 116.8 jit_solution(6568759363793561521)
XLA Ops:
  0.6 0.0 copy-start.5
  0.6 0.0 copy-start.6
  0.7 0.6 copy-done.5
  1.3 0.0 copy-done.6
  1.3 0.0 copy-start
  1.3 1.0 copy-done
  2.3 0.0 copy-start.1
  2.3 1.0 copy-done.1
  3.3 0.0 copy-start.2
  3.3 1.0 copy-done.2
  4.4 0.0 copy-start.3
  4.4 0.8 copy-done.3
  5.2 0.0 copy-start.4
  5.2 0.8 copy-done.4
  6.0 107.3 %shard_map.110 = (bf16[224,128]{1,0:T(8,128)(2,1)S(1)}, f32[1,128]{1,0:T(1,128)S(1)}, bf16[64,3584]{1,0:T(8,128)(2,1)S(1)}, bf16[64,3584]{1,0:T(8,128)(2,1)S(1)}, bf16[64,3584]{1,0:T(8,128)(2,1)S(1)}) custom-call(s32[1,128]{1,0:T(1,128)S(1)} %bitcast.21, bf16[1,128]{1,0:T(2,128)(2,1)S(1)} %bitcast.22, bf16[224,128]{1,0:T(8,128)(2,1)S(1)} %bitcast.19, ...), custom_call_target="tpu_custom_call" | custom-call | tf_op jit(solution)/shard_map/pallas_call | solution.py:386
  113.3 0.6 copy.17
  114.0 0.5 copy.18
  114.5 0.8 copy.19
  115.2 0.8 copy.20
  116.0 0.8 copy.21
Async XLA Ops:
  0.6 0.7 copy-start.5
  0.6 0.7 copy-start.6
  1.3 1.0 copy-start
  2.3 1.0 copy-start.1
  3.3 1.0 copy-start.2
  4.4 0.8 copy-start.3
  5.2 0.8 copy-start.4

commit v2 on v1

v2 whole, which is shorter than its diff:
```python
import functools

import jax
import jax.numpy as jnp
from jax import lax
from jax.experimental import pallas as pl
from jax.experimental.pallas import tpu as pltpu
from jax.sharding import PartitionSpec as P

MESH = pl.DeviceIdType.MESH
BF = jnp.bfloat16
F32 = jnp.float32
NT = (((1,), (1,)), ((), ()))
NN = (((1,), (0,)), ((), ()))
TN = (((0,), (0,)), ((), ()))


def iota(shape, dim):
    return lax.broadcasted_iota(jnp.int32, shape, dim)


def dot(a, b, dims):
    return lax.dot_general(a, b, dims, preferred_element_type=F32)


def pack(left, right):
    lane = iota((96, 128), 1)
    tail = right[96:128]
    moved = jnp.concatenate([pltpu.roll(tail, 96, 1), pltpu.roll(tail, 64, 1), pltpu.roll(tail, 32, 1)], axis=0)
    return jnp.concatenate([left, jnp.where(lane < 96, right[0:96], moved)], axis=0)


def unpack(packed):
    lane = iota((96, 128), 1)
    low = iota((32, 128), 1)
    rest = packed[128:224]
    top = jnp.where(lane < 96, rest, 0.0)
    tail = jnp.where(
        low < 32,
        pltpu.roll(rest[0:32], 32, 1),
        jnp.where(
            low < 64,
            pltpu.roll(rest[32:64], 64, 1),
            jnp.where(low < 96, pltpu.roll(rest[64:96], 96, 1), 0.0),
        ),
    )
    return packed[0:128], jnp.concatenate([top, tail], axis=0)


def shift_left(a, b, count):
    lane = iota(a.shape, 1)
    return jnp.where(lane < 128 - count, pltpu.roll(a, 128 - count, 1), pltpu.roll(b, 128 - count, 1))


def kernel(
    n_dp,
    ids_ref, prob_ref, tok_ref, cot_ref, wg_ref, wu_ref, wd_ref,
    tg_ref, pg_ref, gg_ref, ug_ref, dg_ref,
    sbuf, rbuf, zbuf, wbuf, wpad, tpad, full, gusend, gurecv, bsend, brecv, scal, delt,
    pbx, pbz, pxr, pzr, rs1s, rs1r, rs2s, rs2r, rets, retr, gradb, tokb, cotb, ssem, rsem, lsem,
):
    exp = lax.axis_index("exp")
    me = lax.axis_index("dp")
    x, z = exp // 4, exp % 4
    xs = [(x + k) % 4 for k in range(4)]
    zs = [(z + k) % 4 for k in range(4)]

    def x_dev(k):
        return {"exp": xs[k] * 4 + z, "dp": me}

    def z_dev(k):
        return {"exp": x * 4 + zs[k], "dp": me}

    counter = [0]

    def remote(src, dst, dev):
        i = counter[0]
        counter[0] += 1
        return pltpu.make_async_remote_copy(
            src_ref=src, dst_ref=dst, send_sem=ssem.at[i], recv_sem=rsem.at[i],
            device_id=dev, device_id_type=MESH,
        )

    pending = []

    def start(copy):
        copy.start()
        pending.append(copy)
        return copy

    barrier = pltpu.get_barrier_semaphore()

    def greet(k, carry):
        pl.semaphore_signal(barrier, inc=1, device_id={"exp": exp, "dp": (me + k) % n_dp}, device_id_type=MESH)
        return carry

    lax.fori_loop(1, n_dp, greet, 0)
    for k in range(1, 4):
        pl.semaphore_signal(barrier, inc=1, device_id=x_dev(k), device_id_type=MESH)
        pl.semaphore_signal(barrier, inc=1, device_id=z_dev(k), device_id_type=MESH)

    own_rows = []
    for n, (ref, held) in enumerate(((tok_ref, tokb), (cot_ref, cotb))):
        copy = pltpu.make_async_copy(ref, held, lsem.at[3 + n])
        copy.start()
        own_rows.append(copy)
    own_w = []
    for a, ref in enumerate((wg_ref, wu_ref, wd_ref)):
        copy = pltpu.make_async_copy(
            ref.at[:, pl.ds(pl.multiple_of(x * 896, 128), 896)], wbuf.at[a, x], lsem.at[a]
        )
        copy.start()
        own_w.append(copy)

    ids = ids_ref[...]
    hot = (iota((n_dp, 128), 0) == ids).astype(F32)
    before = (iota((128, 128), 0) < iota((128, 128), 1)).astype(BF)
    earlier = dot(hot.astype(BF), before, NN)
    slot = jnp.sum(hot * earlier, axis=0, keepdims=True)
    position = ids.astype(F32) * 4.0 + slot

    rows = iota((16 * n_dp, 128), 0)
    row_slot = ((rows >> 4) * 4 + (rows & 3)).astype(F32)
    row_part = (rows >> 2) & 3
    placing = jnp.where(row_slot == position, 1.0, 0.0).astype(BF)
    prob_block = jnp.where(iota((32, 128), 0) == 0, prob_ref[...].astype(F32), 0.0).astype(BF)
    for copy in own_rows:
        copy.wait()
    out = dot(placing, tokb[0:128], NT)
    out = jnp.where(row_part == 1, dot(placing, jnp.concatenate([tokb[128:224], prob_block], axis=0), NT), out)
    out = jnp.where(row_part == 2, dot(placing, cotb[0:128], NT), out)
    zero_block = jnp.zeros((32, 128), BF)
    out = jnp.where(row_part == 3, dot(placing, jnp.concatenate([cotb[128:224], zero_block], axis=0), NT), out)
    sbuf[...] = out.astype(BF).reshape(n_dp, 16, 128)

    pl.semaphore_wait(barrier, n_dp - 1 + 6)

    i_disp = counter[0]
    counter[0] += 1

    def send(k, carry):
        to = (me + k) % n_dp
        pltpu.make_async_remote_copy(
            src_ref=sbuf.at[to], dst_ref=rbuf.at[me], send_sem=ssem.at[i_disp], recv_sem=rsem.at[i_disp],
            device_id={"exp": exp, "dp": to}, device_id_type=MESH,
        ).start()
        return carry

    lax.fori_loop(1, n_dp, send, 0)
    rbuf[me] = sbuf[me]

    w_copies = [
        [
            start(remote(
                ref.at[:, pl.ds(pl.multiple_of(xs[k] * 896, 128), 896)], wbuf.at[a, x], x_dev(k)
            ))
            for k in range(1, 4)
        ]
        for a, ref in enumerate((wg_ref, wu_ref, wd_ref))
    ]

    dispatched = pltpu.make_async_remote_copy(
        src_ref=sbuf.at[pl.ds(0, n_dp - 1)], dst_ref=rbuf.at[pl.ds(0, n_dp - 1)],
        send_sem=ssem.at[i_disp], recv_sem=rsem.at[i_disp], device_id={"exp": exp, "dp": me}, device_id_type=MESH,
    )
    dispatched.wait_recv()

    o, i = iota((256, 256), 0), iota((256, 256), 1)
    order = jnp.where(i == ((o >> 2) & 15) * 16 + (o >> 6) * 4 + (o & 3), 1.0, 0.0).astype(BF)
    groups = []
    for g in range(n_dp // 16):
        groups.append(dot(order, rbuf[16 * g:16 * g + 16].reshape(256, 128), NN))
    parts = [jnp.concatenate([group[64 * j:64 * j + 64] for group in groups], axis=0) for j in range(4)]
    pick = jnp.where((iota((8, 128), 0) == 0) & (iota((8, 128), 1) == 96), 1.0, 0.0).astype(BF)
    weight = dot(pick, parts[1].astype(BF), NT)[0:1]

    def gather_start(h, a):
        mine = zbuf.at[h, a, z]
        halves = [mine.at[pl.ds(0, 112)], mine.at[pl.ds(112, 112)]]
        right = [remote(halves[0], halves[0], z_dev(1)), remote(halves[1], halves[1], z_dev(1))]
        left = [remote(halves[1], halves[1], z_dev(3)), remote(halves[0], halves[0], z_dev(3))]
        for n in range(2):
            start(right[n])
            start(left[n])
        return right, left

    def gather_forward(h, a, right, left):
        from_left = zbuf.at[h, a, zs[3], pl.ds(0, 112)]
        from_right = zbuf.at[h, a, zs[1], pl.ds(112, 112)]
        onward_right = remote(from_left, from_left, z_dev(1))
        onward_left = remote(from_right, from_right, z_dev(3))
        right[0].wait_recv()
        start(onward_right)
        left[0].wait_recv()
        start(onward_left)
        return [right[1], left[1], onward_right, onward_left]

    def gather_rest(copies):
        for copy in copies:
            copy.wait_recv()

    for h in range(2):
        half = slice(128 * h, 128 * h + 128)
        for a in range(2):
            zbuf[h, a, z] = pack(parts[2 * a][half], parts[2 * a + 1][half]).astype(BF)
            if h == 0 and a == 0:
                t0 = gather_start(0, 0)

    def shift_weights(a):
        own_w[a].wait()
        for copy in w_copies[a]:
            copy.wait_recv()
        whole = wbuf[a].reshape(256, 896)
        block = [whole[:, 128 * b:128 * b + 128].astype(F32) for b in range(7)]
        wpad[a, 0] = whole[:, 0:256]
        for n, (first, count) in enumerate(((1, 96), (3, 64), (5, 32))):
            wpad[a, n + 1, :, 0:128] = shift_left(block[first], block[first + 1], count).astype(BF)
            last = block[first + 2] if first + 2 < 7 else block[first + 1]
            wpad[a, n + 1, :, 128:256] = shift_left(block[first + 1], last, count).astype(BF)

    def unpack_all(h, a):
        for n in range(4):
            left, right = unpack(zbuf[h, a, n].astype(F32))
            tpad[a, n, 128 * h:128 * h + 128, 0:128] = left.astype(BF)
            tpad[a, n, 128 * h:128 * h + 128, 128:256] = right.astype(BF)

    def join_all(a):
        part = [[tpad[a, n, :, 128 * h:128 * h + 128].astype(F32) for h in range(2)] for n in range(4)]
        nothing = jnp.zeros((256, 128), F32)
        block = [nothing] * 7
        block[0], block[1] = part[0]
        for n, (first, count) in enumerate(((1, 96), (3, 64), (5, 32))):
            lo, hi = part[n + 1]
            block[first] += shift_left(nothing, lo, 128 - count)
            block[first + 1] += shift_left(lo, hi, 128 - count)
            if first + 2 < 7:
                block[first + 2] += shift_left(hi, nothing, 128 - count)
        for b in range(7):
            full[a, :, 128 * b:128 * b + 128] = block[b].astype(BF)

    def project(h, a, t):
        rows_of = slice(128 * h, 128 * h + 128)
        total = dot(wpad[a, 0], tpad[t, 0, rows_of], NT)
        for n in range(1, 4):
            total += dot(wpad[a, n], tpad[t, n, rows_of], NT)
        return total.reshape(4, 64, 128)

    def to_x(src, dst):
        return [start(remote(src(k), dst(k), x_dev(k))) for k in range(1, 4)]

    def forward_rows(h):
        unpack_all(h, 0)
        gusend[h, :, 0] = project(h, 0, 0)
        gusend[h, :, 1] = project(h, 1, 0)
        return to_x(lambda k: gusend.at[h, xs[k]], lambda k: gurecv.at[h, k - 1])

    def backward_rows(h):
        unpack_all(h, 1)
        bsend[h] = project(h, 2, 1)
        return to_x(lambda k: bsend.at[h, xs[k]], lambda k: brecv.at[h, k - 1])

    def activate(h, copies):
        gather_rest(copies)
        gate = gusend[h, x, 0] + gurecv[h, 0, 0] + gurecv[h, 1, 0] + gurecv[h, 2, 0]
        upper = gusend[h, x, 1] + gurecv[h, 0, 1] + gurecv[h, 1, 1] + gurecv[h, 2, 1]
        sigmoid = jax.nn.sigmoid(gate)
        hidden = gate * sigmoid * upper
        scal[h, x] = (weight[:, 128 * h:128 * h + 128] * hidden).astype(BF)
        sent = to_x(lambda k: scal.at[h, x], lambda k: scal.at[h, x])
        return sent, gate, upper, sigmoid, hidden

    def deltas(h, copies, gate, upper, sigmoid, hidden):
        gather_rest(copies)
        back = bsend[h, x] + brecv[h, 0] + brecv[h, 1] + brecv[h, 2]
        grad = weight[:, 128 * h:128 * h + 128] * back
        delt[h, 0, x] = (grad * upper * sigmoid * (1.0 + gate * (1.0 - sigmoid))).astype(BF)
        delt[h, 1, x] = (grad * gate * sigmoid).astype(BF)
        sent = to_x(lambda k: delt.at[h, :, x], lambda k: delt.at[h, :, x])
        pbx[h] = jnp.broadcast_to(jnp.sum(hidden * back, axis=0, keepdims=True), (8, 128))
        return sent, to_x(lambda k: pbx.at[h], lambda k: pxr.at[h, k - 1])

    def token_part(h, n):
        total = dot(delt[h, 0].reshape(256, 128), wpad[0, n], TN) + dot(delt[h, 1].reshape(256, 128), wpad[1, n], TN)
        return pack(total[:, 0:128], total[:, 128:256])

    def scatter_start(h, copies, prob_copies):
        gather_rest(copies)
        rs1s[h] = token_part(h, zs[2]).astype(BF).reshape(2, 112, 128)
        first = [
            start(remote(rs1s.at[h, 0], rs1r.at[h, 0], z_dev(1))),
            start(remote(rs1s.at[h, 1], rs1r.at[h, 1], z_dev(3))),
        ]
        to_right = token_part(h, zs[1])
        rs2s[h, 0, 1] = to_right[112:224].astype(BF)
        second = [start(remote(rs2s.at[h, 0, 1], rs2r.at[h, 0, 1], z_dev(1)))]
        to_left = token_part(h, zs[3])
        rs2s[h, 1, 0] = to_left[0:112].astype(BF)
        second.append(start(remote(rs2s.at[h, 1, 0], rs2r.at[h, 1, 0], z_dev(3))))
        gather_rest(prob_copies)
        pbz[h] = pbx[h] + pxr[h, 0] + pxr[h, 1] + pxr[h, 2]
        prob = [start(remote(pbz.at[h], pzr.at[h, k - 1], z_dev(k))) for k in range(1, 4)]
        return first, second, prob, to_right, to_left

    def scatter_on(h, first, second, to_right, to_left):
        first[0].wait_recv()
        rs2s[h, 0, 0] = (to_right[0:112] + rs1r[h, 0].astype(F32)).astype(BF)
        second.append(start(remote(rs2s.at[h, 0, 0], rs2r.at[h, 0, 0], z_dev(1))))
        first[1].wait_recv()
        rs2s[h, 1, 1] = (to_left[112:224] + rs1r[h, 1].astype(F32)).astype(BF)
        second.append(start(remote(rs2s.at[h, 1, 1], rs2r.at[h, 1, 1], z_dev(3))))

    i_ret = counter[0]
    counter[0] += 1
    o, i = iota((128, 128), 0), iota((128, 128), 1)
    back_order = jnp.where(i == ((o >> 2) & 1) * 64 + (o >> 3) * 4 + (o & 3), 1.0, 0.0).astype(BF)
    into = jnp.where(
        (iota((8, 128), 0) < 3) & (iota((8, 128), 1) == iota((8, 128), 0) + 96), 1.0, 0.0
    ).astype(BF)

    def finish_rows(h, here, second, prob):
        gather_rest(prob)
        total = (pbz[h] + pzr[h, 0] + pzr[h, 1] + pzr[h, 2])[0:1]
        high = total.astype(BF).astype(F32)
        middle = (total - high).astype(BF).astype(F32)
        low = total - high - middle
        eight = iota((8, 128), 0)
        terms = jnp.where(eight == 0, high, jnp.where(eight == 1, middle, jnp.where(eight == 2, low, 0.0))).astype(BF)
        prob_lanes = dot(terms, into, TN)
        gather_rest(second)
        both = rs2r[h, 0].astype(F32) + rs2r[h, 1].astype(F32)
        left, right = unpack(here + both.reshape(224, 128))
        left = left.astype(BF)
        right = (right + prob_lanes).astype(BF)
        count = n_dp // 2
        for g in range(2):
            piece = jnp.concatenate([left[64 * g:64 * g + 64], right[64 * g:64 * g + 64]], axis=0)
            rets[count * h + 16 * g:count * h + 16 * g + 16] = dot(back_order, piece, NN).reshape(16, 8, 128)

        def send_back(k, carry):
            to = h * count + (me + k) % count

            @pl.when(to != me)
            def _():
                pltpu.make_async_remote_copy(
                    src_ref=rets.at[to], dst_ref=retr.at[me], send_sem=ssem.at[i_ret], recv_sem=rsem.at[i_ret],
                    device_id={"exp": exp, "dp": to}, device_id_type=MESH,
                ).start()

            return carry

        lax.fori_loop(0, count, send_back, 0)

    c0 = gather_start(0, 1)
    shift_weights(0)
    t0_rest = gather_forward(0, 0, *t0)
    t1 = gather_start(1, 0)
    shift_weights(1)
    c0_rest = gather_forward(0, 1, *c0)
    c1 = gather_start(1, 1)
    gather_rest(t0_rest)
    gu0 = forward_rows(0)
    shift_weights(2)
    t1_rest = gather_forward(1, 0, *t1)
    gather_rest(c0_rest)
    b0 = backward_rows(0)
    s0, *kept0 = activate(0, gu0)
    c1_rest = gather_forward(1, 1, *c1)
    d0, p0 = deltas(0, b0, *kept0)
    gather_rest(t1_rest)
    gu1 = forward_rows(1)
    first0, second0, prob0, to_right0, to_left0 = scatter_start(0, d0, p0)
    gather_rest(c1_rest)
    b1 = backward_rows(1)
    s1, *kept1 = activate(1, gu1)
    scatter_on(0, first0, second0, to_right0, to_left0)
    here0 = token_part(0, z)
    d1, p1 = deltas(1, b1, *kept1)
    join_all(0)
    first1, second1, prob1, to_right1, to_left1 = scatter_start(1, d1, p1)
    finish_rows(0, here0, second0, prob0)
    join_all(1)
    scatter_on(1, first1, second1, to_right1, to_left1)
    here1 = token_part(1, z)

    def grad_send(a, lhs, t, ref):
        total = dot(lhs[0].reshape(256, 128), full[t, 0:128], NN) + dot(lhs[1].reshape(256, 128), full[t, 128:256], NN)
        gradb[a] = total.astype(BF).reshape(4, 64, 896)
        lanes = pl.ds(pl.multiple_of(x * 896, 128), 896)
        sent = to_x(lambda k: gradb.at[a, xs[k]], lambda k: ref.at[:, lanes])
        ref[:, lanes] = gradb[a, x]
        return sent

    gather_rest(s0 + s1)
    g_copies = grad_send(2, [scal[0], scal[1]], 1, dg_ref)
    g_copies += grad_send(0, [delt[0, 0], delt[1, 0]], 0, gg_ref)
    g_copies += grad_send(1, [delt[0, 1], delt[1, 1]], 0, ug_ref)
    finish_rows(1, here1, second1, prob1)
    retr[me] = rets[me]
    rows = iota((8 * n_dp, 128), 0)
    match = ((rows >> 3) * 4 + (rows & 3)).astype(F32) == position
    part = (rows >> 2) & 1
    returned = pltpu.make_async_remote_copy(
        src_ref=rets.at[pl.ds(0, n_dp - 1)], dst_ref=retr.at[pl.ds(0, n_dp - 1)],
        send_sem=ssem.at[i_ret], recv_sem=rsem.at[i_ret], device_id={"exp": exp, "dp": me}, device_id_type=MESH,
    )
    returned.wait_recv()
    arrived = retr[...].reshape(8 * n_dp, 128)
    small = arrived.astype(BF)
    tg_ref[0:128] = dot(small, jnp.where(match & (part == 0), 1.0, 0.0).astype(BF), TN).astype(BF)
    tg_ref[128:224] = dot(small, jnp.where(match & (part == 1), 1.0, 0.0).astype(BF), TN)[0:96].astype(BF)
    column = arrived[:, 96:97] + arrived[:, 97:98] + arrived[:, 98:99]
    pg_ref[...] = jnp.sum(jnp.where(match & (part == 1), column, 0.0), axis=0, keepdims=True)

    for copy in g_copies:
        copy.wait_recv()
    dispatched.wait_send()
    returned.wait_send()
    for copy in pending:
        copy.wait_send()


def hand_over(*refs):
    count = len(refs) // 2
    copies = [pltpu.make_async_copy(refs[n], refs[count + n], refs[-1].at[n]) for n in range(count)]
    for copy in copies:
        copy.start()
    for copy in copies:
        copy.wait()


def shards(tokens, cotangent, expert_ids, gate_prob, w_gate, w_up, w_down):
    n_dp = lax.axis_size("dp")
    vmem = pl.BlockSpec(memory_space=pltpu.VMEM)
    hbm = pl.BlockSpec(memory_space=pl.ANY)
    grad = jax.ShapeDtypeStruct((64, 3584), BF)
    made = pl.pallas_call(
        functools.partial(kernel, n_dp),
        out_shape=(
            jax.ShapeDtypeStruct((224, 128), BF),
            jax.ShapeDtypeStruct((1, 128), F32),
            grad, grad, grad,
        ),
        in_specs=[vmem] * 2 + [hbm] * 5,
        out_specs=[vmem] * 5,
        scratch_shapes=[
            pltpu.VMEM((n_dp, 16, 128), BF),
            pltpu.VMEM((n_dp, 16, 128), BF),
            pltpu.VMEM((2, 2, 4, 224, 128), BF),
            pltpu.VMEM((3, 4, 64, 896), BF),
            pltpu.VMEM((3, 4, 256, 256), BF),
            pltpu.VMEM((2, 4, 256, 256), BF),
            pltpu.VMEM((2, 256, 896), BF),
            pltpu.VMEM((2, 4, 2, 64, 128), F32),
            pltpu.VMEM((2, 3, 2, 64, 128), F32),
            pltpu.VMEM((2, 4, 64, 128), F32),
            pltpu.VMEM((2, 3, 64, 128), F32),
            pltpu.VMEM((2, 4, 64, 128), BF),
            pltpu.VMEM((2, 2, 4, 64, 128), BF),
            pltpu.VMEM((2, 8, 128), F32),
            pltpu.VMEM((2, 8, 128), F32),
            pltpu.VMEM((2, 3, 8, 128), F32),
            pltpu.VMEM((2, 3, 8, 128), F32),
            pltpu.VMEM((2, 2, 112, 128), BF),
            pltpu.VMEM((2, 2, 112, 128), BF),
            pltpu.VMEM((2, 2, 2, 112, 128), BF),
            pltpu.VMEM((2, 2, 2, 112, 128), BF),
            pltpu.VMEM((n_dp, 8, 128), F32),
            pltpu.VMEM((n_dp, 8, 128), F32),
            pltpu.VMEM((3, 4, 64, 896), BF),
            pltpu.VMEM((224, 128), BF),
            pltpu.VMEM((224, 128), BF),
            pltpu.SemaphoreType.DMA((96,)),
            pltpu.SemaphoreType.DMA((96,)),
            pltpu.SemaphoreType.DMA((5,)),
        ],
        compiler_params=pltpu.CompilerParams(
            collective_id=0, has_side_effects=True, vmem_limit_bytes=60 * 1024 * 1024
        ),
    )(
        expert_ids.reshape(1, -1), gate_prob.reshape(1, -1), tokens.T, cotangent.T, w_gate[0], w_up[0], w_down[0]
    )
    token_grad, prob_grad, gate_grad, up_grad, down_grad = pl.pallas_call(
        hand_over,
        out_shape=tuple(jax.ShapeDtypeStruct(array.shape, array.dtype) for array in made),
        in_specs=[hbm] * 5,
        out_specs=[hbm] * 5,
        scratch_shapes=[pltpu.SemaphoreType.DMA((5,))],
        compiler_params=pltpu.CompilerParams(vmem_limit_bytes=60 * 1024 * 1024),
    )(*made)
    return token_grad.T, prob_grad.reshape(-1), gate_grad[None], up_grad[None], down_grad[None]


def solution(mesh):
    in_specs = (
        P("dp", "exp"),
        P("dp", "exp"),
        P("dp", None),
        P("dp"),
        P("dp", "exp", None),
        P("dp", "exp", None),
        P("dp", "exp", None),
    )
    out_specs = (
        P("dp", "exp"),
        P("dp"),
        P("dp", "exp", None),
        P("dp", "exp", None),
        P("dp", "exp", None),
    )
    return jax.shard_map(shards, mesh=mesh, in_specs=in_specs, out_specs=out_specs, check_vma=False)
```

time: 117 us -> 153 us (1.31)
  the two profiles are of different devices: /device:TPU:1 before, /device:TPU:16 now
where the time goes in v2:
time: 153 us
  Pallas kernels  152 us (99%)
    pallas_call x1, Pallas kernels, shards(): pl.pallas_call(functools.partial(kernel, n_dp), out_shape=(jax.ShapeDtype...  107 us
    pallas_call x1, Pallas kernels, shards(): pl.pallas_call(hand_over, out_shape=tuple((jax.ShapeDtypeStruct(array.sha...  44.6 us

profile of v2, /device:TPU:16, one launch (start us, length us, event | category | flops | bytes accessed | tf_op | source)
XLA Modules:
  0.0 152.7 jit_solution(2746772712805927106)
XLA Ops:
  0.6 107.5 %shard_map.110 = (bf16[224,128]{1,0:T(8,128)(2,1)}, f32[1,128]{1,0:T(1,128)}, bf16[64,3584]{1,0:T(8,128)(2,1)}, bf16[64,3584]{1,0:T(8,128)(2,1)}, bf16[64,3584]{1,0:T(8,128)(2,1)}) custom-call(s32[1,128]{1,0:T(1,128)} %bitcast.17, bf16[1,128]{1,0:T(2,128)(2,1)} %bitcast.18, bf16[224,128]{1,0:T(8,128)(2,1)} %bitcast.15, bf16[224,128]{1,0:T(8,128)(2,1)} %bitcast.16, ...), custom_call_target="tpu_custom_call" | custom-call | tf_op jit(solution)/shard_map/pallas_call | solution.py:436
  108.1 44.6 %shard_map.111 = (bf16[224,128]{1,0:T(8,128)(2,1)}, f32[1,128]{1,0:T(1,128)}, bf16[64,3584]{1,0:T(8,128)(2,1)}, bf16[64,3584]{1,0:T(8,128)(2,1)}, bf16[64,3584]{1,0:T(8,128)(2,1)}) custom-call(bf16[224,128]{1,0:T(8,128)(2,1)} %get-tuple-element.15.refs_0_, f32[1,128]{1,0:T(1,128)} %get-tuple-element.16.refs_1_, bf16[64,3584]{1,0:T(8,128)(2,1)} %get-tuple-element.17.refs_2_, ...), custom_call_target="tpu_custom_call" | custom-call | tf_op jit(solution)/shard_map/pallas_call | solution.py:482
